TPU v7x, 32 devices: a whole 2x2x4 slice. The times are simulated.
32 devices in a mesh: chan: 16 (over z, x, core), win: 2 (over y).
Axes of the slice: x: 2, y: 2, z: 4, core: 2. Of those that a mesh axis runs over, the one named last changes fastest.
Arguments:
- strain_rate: bfloat16 [2, 1024, 8192], P('win', 'chan'), may hold values from -600 to 600
- bandpass_taps: bfloat16 [65], replicated, may hold values from -0.75 to 0.75
- pair_offsets: int32 [16, 6], P('chan'), may hold values from -1 to 15, as said below
- lag_limit: int32 [16, 6], P('chan'), may hold values from 1 to 8
Outputs:
- correlations: float32 [6, 8192, 2176], P(None, ('chan', 'win'))
Inputs may be any that keep to these rules, and one draw needn't show every extreme that they name: `pair_offsets`: row b lists distinct block offsets o (partner block (b + o) mod 16) in its first slots and -1 in the remaining slots; every row has at least one offset, some row uses all 6 slots and some row only one.
All inputs are finite; a program needn't handle non-finite values.
Results may differ from a plain program's by a relative error of at most 0.0027.
Values may be sent and summed in bfloat16 or wider, within the bound.
A program may use at most 128 MiB of HBM per device.

v0:
```python
import functools
import math

import jax
import jax.numpy as jnp
from jax import lax
from jax.experimental import pallas as pl
from jax.experimental.pallas import tpu as pltpu
from jax.sharding import PartitionSpec as P

VIRTUAL_SOURCES = 128
MAXIMUM_LAG = 8
LAGS = 2 * MAXIMUM_LAG + 1
PIECE = 256
REACH = 384
LAG_ORDER = sorted(range(-MAXIMUM_LAG, MAXIMUM_LAG + 1), key=abs)
NEAR = 9
VMEM_LIMIT = 56 * 1024 * 1024


def band(row, half):
    wide = jnp.broadcast_to(row, (PIECE, REACH))
    return pltpu.roll(wide, 0, 1, stride=1, stride_axis=0).astype(jnp.bfloat16)


def normalize_kernel(half, taps_ref, x_ref, out_ref, src_ref, padded, level, filtered):
    parts, _, rows, channels = x_ref.shape
    samples = parts * rows
    tap_count = 2 * half + 1
    tail = padded.shape[0] - samples - half
    padded[:half] = jnp.zeros((half, channels), jnp.bfloat16)
    padded[half + samples :] = jnp.zeros((tail, channels), jnp.bfloat16)
    level[:half] = jnp.zeros((half, channels), jnp.bfloat16)
    level[half + samples :] = jnp.zeros((tail, channels), jnp.bfloat16)
    for i in range(parts):
        padded[half + i * rows : half + (i + 1) * rows] = x_ref[i, 0]
    taps = band(taps_ref[...], half)
    ones = jnp.where(
        lax.broadcasted_iota(jnp.int32, (1, REACH), 1) < tap_count, 1.0, 0.0
    ).astype(jnp.float32)
    box = band(ones, half)
    for p in range(samples // PIECE):
        low = p * PIECE
        value = jnp.dot(taps, padded[low : low + REACH], preferred_element_type=jnp.float32)
        filtered[low : low + PIECE] = value
        level[half + low : half + low + PIECE] = jnp.abs(value).astype(jnp.bfloat16)
    per = src_ref.shape[0]
    spacing = channels // per
    pick = (
        lax.broadcasted_iota(jnp.int32, (per, channels), 1)
        == spacing * lax.broadcasted_iota(jnp.int32, (per, channels), 0)
    )
    pick = jnp.where(pick, 1.0, 0.0).astype(jnp.bfloat16)
    for p in range(samples // PIECE):
        low = p * PIECE
        total = jnp.dot(box, level[low : low + REACH], preferred_element_type=jnp.float32)
        mean = total * (1.0 / tap_count)
        value = filtered[low : low + PIECE] / (mean + 1e-05)
        turned = jnp.transpose(value).astype(jnp.bfloat16)
        out_ref[:, low : low + PIECE] = turned
        src_ref[:, low : low + PIECE] = jnp.dot(
            pick, turned, preferred_element_type=jnp.float32
        ).astype(jnp.bfloat16)


def normalize(parts, taps):
    blocks, windows, rows, channels = parts.shape
    samples = blocks * rows
    half = (taps.shape[0] - 1) // 2
    sources = VIRTUAL_SOURCES // windows
    row = jnp.pad(taps.astype(jnp.float32), (0, REACH - taps.shape[0]))[None]
    return pl.pallas_call(
        functools.partial(normalize_kernel, half),
        grid=(windows,),
        out_shape=(
            jax.ShapeDtypeStruct((channels, windows * samples), jnp.bfloat16),
            jax.ShapeDtypeStruct((sources, windows * samples), jnp.bfloat16),
        ),
        in_specs=[
            pl.BlockSpec((1, REACH), lambda w: (0, 0)),
            pl.BlockSpec((blocks, 1, rows, channels), lambda w: (0, w, 0, 0)),
        ],
        out_specs=(
            pl.BlockSpec((channels, samples), lambda w: (0, w)),
            pl.BlockSpec((sources, samples), lambda w: (0, w)),
        ),
        scratch_shapes=[
            pltpu.VMEM((samples + REACH - PIECE, channels), jnp.bfloat16),
            pltpu.VMEM((samples + REACH - PIECE, channels), jnp.bfloat16),
            pltpu.VMEM((samples, channels), jnp.float32),
        ],
        compiler_params=pltpu.CompilerParams(vmem_limit_bytes=VMEM_LIMIT),
        name="normalize",
    )(row, parts)


def moved_rows(value, spot, lag):
    samples = value.shape[1]
    if lag == 0:
        return value
    kept = spot >= lag if lag > 0 else spot < samples + lag
    return jnp.where(kept, pltpu.roll(value, lag % samples, 1), 0.0)


def shift_kernel(x_ref, out_ref):
    rows, samples = x_ref.shape
    value = x_ref[...].astype(jnp.float32)
    spot = lax.broadcasted_iota(jnp.int32, (rows, samples), 1)
    for index, lag in enumerate(LAG_ORDER):
        out_ref[index] = moved_rows(value, spot, lag).astype(jnp.bfloat16)


def shift(receivers, windows):
    channels, length = receivers.shape
    samples = length // windows
    rows = min(32, channels)
    return pl.pallas_call(
        shift_kernel,
        grid=(channels // rows, windows),
        out_shape=jax.ShapeDtypeStruct((LAGS, channels, length), jnp.bfloat16),
        in_specs=[pl.BlockSpec((rows, samples), lambda c, w: (c, w))],
        out_specs=pl.BlockSpec((LAGS, rows, samples), lambda c, w: (0, c, w)),
        compiler_params=pltpu.CompilerParams(vmem_limit_bytes=VMEM_LIMIT),
        name="shift",
    )(receivers)


def when(present, action):
    if present is None:
        action()
    else:
        pl.when(present)(action)


def gather_kernel(
    line, windows, src_ref, x_ref, out_ref, lagged_ref, held, local_sem, send_sem, recv_sem, out_sem
):
    chan, win = lax.axis_index("chan"), lax.axis_index("win")
    z, x, core = chan // 4, (chan // 2) % 2, chan % 2
    first_x = x + (1 - core) * (1 - 2 * x)
    first_win = win + core * (1 - 2 * win)
    second_x = x + core * (1 - 2 * x)
    second_win = win + (1 - core) * (1 - 2 * win)

    def device(z, x, core, win):
        return (z * 4 + x * 2 + core, win)

    def block(z, x, core, win):
        return (z * 4 + x * 2 + core) * 2 + win

    first = device(z, first_x, core, first_win)
    second = device(z, second_x, core, second_win)
    sibling = device(z, x, 1 - core, win)
    up, down = device(z + 1, x, core, win), device(z - 1, x, core, win)
    has_up, has_down = z + 1 < line, z >= 1

    barrier = pltpu.get_barrier_semaphore()

    def greet(partner):
        pl.semaphore_signal(
            barrier, inc=1, device_id=partner, device_id_type=pl.DeviceIdType.MESH
        )

    for partner in (first, second, sibling):
        greet(partner)
    when(has_up, functools.partial(greet, up))
    when(has_down, functools.partial(greet, down))
    levels_beside = (z + line - 1) // line + (2 * line - 2 - z) // line
    pl.semaphore_wait(barrier, 3 + levels_beside)

    started = []

    def send(target, number, present, own=False):
        copy = pltpu.make_async_remote_copy(
            src_ref=src_ref if own else out_ref.at[number],
            dst_ref=out_ref.at[number],
            send_sem=send_sem.at[len(started)],
            recv_sem=recv_sem.at[number],
            device_id=target,
            device_id_type=pl.DeviceIdType.MESH,
        )
        started.append((present, copy))
        when(present, copy.start)

    def arrived(number):
        pltpu.make_async_remote_copy(
            src_ref=out_ref.at[number],
            dst_ref=out_ref.at[number],
            send_sem=send_sem.at[0],
            recv_sem=recv_sem.at[number],
            device_id=sibling,
            device_id_type=pl.DeviceIdType.MESH,
        ).wait_recv()

    lags, rows, length = held.shape[1:]
    samples = length // windows
    chunks = x_ref.shape[0] // rows
    spot = lax.broadcasted_iota(jnp.int32, (rows, samples), 1)

    def write(slot, chunk):
        return pltpu.make_async_copy(
            held.at[slot],
            lagged_ref.at[:, pl.ds(pl.multiple_of(chunk * rows, rows), rows), :],
            out_sem.at[slot],
        )

    def shift_chunk(chunk, carry):
        slot = chunk % 2

        @pl.when(chunk >= 2)
        def _():
            write(slot, chunk - 2).wait()

        for w in range(windows):
            part = x_ref[
                pl.ds(pl.multiple_of(chunk * rows, rows), rows), w * samples : (w + 1) * samples
            ].astype(jnp.float32)
            for index, lag in enumerate(LAG_ORDER):
                held[slot, index, :, w * samples : (w + 1) * samples] = moved_rows(
                    part, spot, lag
                ).astype(jnp.bfloat16)
        write(slot, chunk).start()
        return carry

    own = block(z, x, core, win)
    mine = pltpu.make_async_copy(src_ref, out_ref.at[own], local_sem)
    send(up, own, has_up, own=True)
    send(down, own, has_down, own=True)
    for target in (first, second, sibling):
        send(target, own, None, own=True)
    mine.start()
    levels = [(z, None)]
    for r in range(1, line):
        levels += [(z - r, z >= r), (z + r, z + r < line)]
    done = 0
    for index, (level, present) in enumerate(levels):
        if index > 0:
            number = block(level, x, core, win)
            when(present, functools.partial(arrived, number))
            if index % 2 == 1:
                onward = jnp.logical_and(present, has_up)
                send(up, number, onward)
            else:
                onward = jnp.logical_and(present, has_down)
                send(down, number, onward)
            for target in (first, second, sibling):
                send(target, number, present)
        for step, (px, pwin) in enumerate(
            [(first_x, first_win), (second_x, second_win), (1 - x, 1 - win)]
        ):
            if done < chunks:
                lax.fori_loop(done, done + 1, shift_chunk, 0)
                done += 1
            number = block(level, px, core, pwin)
            when(present, functools.partial(arrived, number))
            if step == 0:
                send(second, number, present)
            send(sibling, number, present)
    if done < chunks:
        lax.fori_loop(done, chunks, shift_chunk, 0)
    for level in range(line):
        for px, pwin in [(x, win), (first_x, first_win), (second_x, second_win), (1 - x, 1 - win)]:
            arrived(block(level, px, 1 - core, pwin))
    for chunk in range(max(0, chunks - 2), chunks):
        write(chunk % 2, chunk).wait()
    mine.wait()
    for present, copy in started:
        when(present, copy.wait_send)


def gather_and_shift(sources, receivers, blocks, windows):
    line = blocks // 4
    channels, length = receivers.shape
    rows = 16
    devices = blocks * windows
    whole = pl.BlockSpec(memory_space=pl.ANY)
    gathered, lagged = pl.pallas_call(
        functools.partial(gather_kernel, line, windows),
        out_shape=(
            jax.ShapeDtypeStruct((devices, *sources.shape), jnp.bfloat16),
            jax.ShapeDtypeStruct((LAGS, channels, length), jnp.bfloat16),
        ),
        in_specs=[whole, pl.BlockSpec(memory_space=pltpu.VMEM)],
        out_specs=(whole, whole),
        scratch_shapes=[
            pltpu.VMEM((2, LAGS, rows, length), jnp.bfloat16),
            pltpu.SemaphoreType.DMA,
            pltpu.SemaphoreType.DMA((16 * line,)),
            pltpu.SemaphoreType.DMA((devices,)),
            pltpu.SemaphoreType.DMA((2,)),
        ],
        compiler_params=pltpu.CompilerParams(
            collective_id=0, has_side_effects=True, vmem_limit_bytes=VMEM_LIMIT
        ),
        name="gather_and_shift",
    )(sources, receivers)
    return gathered.reshape(blocks, VIRTUAL_SOURCES, length), lagged


def correlate_kernel(factor, partner, limit, lhs_ref, *refs):
    source_refs, out_ref = refs[:-1], refs[-1]
    slots = len(source_refs)
    _, rows, length = lhs_ref.shape

    def columns(index):
        low = (LAG_ORDER[index] + MAXIMUM_LAG) * VIRTUAL_SOURCES
        return slice(low, low + VIRTUAL_SOURCES)

    def multiply(group, low, high):
        panel = jnp.concatenate([source_refs[k][0] for k in group], axis=0)
        product = lax.dot_general(
            lhs_ref[low:high].reshape((high - low) * rows, length),
            panel,
            (((1,), (1,)), ((), ())),
            preferred_element_type=jnp.float32,
        )
        for index in range(low, high):
            for i, k in enumerate(group):
                piece = product[
                    (index - low) * rows : (index - low + 1) * rows,
                    i * VIRTUAL_SOURCES : (i + 1) * VIRTUAL_SOURCES,
                ]
                kept = abs(LAG_ORDER[index]) <= limit[k]
                out_ref[k, :, columns(index)] = jnp.where(kept, piece * factor, 0.0)

    def clear(group, low, high):
        for index in range(low, high):
            for k in group:
                out_ref[k, :, columns(index)] = jnp.zeros((rows, VIRTUAL_SOURCES), jnp.float32)

    for first in range(0, slots, 2):
        group = range(first, min(first + 2, slots))
        reach = functools.reduce(jnp.maximum, [limit[k] for k in group])
        for low, high in ((0, NEAR), (NEAR, LAGS)):
            needed = reach >= abs(LAG_ORDER[low])
            pl.when(needed)(functools.partial(multiply, group, low, high))
            pl.when(jnp.logical_not(needed))(functools.partial(clear, group, low, high))


def correlate(lagged, gathered, partner, limit):
    _, channels, length = lagged.shape
    slots = partner.shape[0]
    rows = min(64, channels)

    def source_spec(k):
        return pl.BlockSpec(
            (1, VIRTUAL_SOURCES, length), lambda c, partner, limit: (partner[k], 0, 0)
        )

    return pl.pallas_call(
        functools.partial(correlate_kernel, 1.0 / math.sqrt(length)),
        grid_spec=pltpu.PrefetchScalarGridSpec(
            num_scalar_prefetch=2,
            grid=(channels // rows,),
            in_specs=[pl.BlockSpec((LAGS, rows, length), lambda c, partner, limit: (0, c, 0))]
            + [source_spec(k) for k in range(slots)],
            out_specs=pl.BlockSpec(
                (slots, rows, LAGS * VIRTUAL_SOURCES), lambda c, partner, limit: (0, c, 0)
            ),
        ),
        out_shape=jax.ShapeDtypeStruct((slots, channels, LAGS * VIRTUAL_SOURCES), jnp.float32),
        compiler_params=pltpu.CompilerParams(vmem_limit_bytes=VMEM_LIMIT),
        name="correlate",
    )(partner, limit, lagged, *[gathered] * slots)


def gather_by_window(sources, partner, windows):
    samples = sources.shape[1] // windows
    blocks = lax.axis_size("chan")

    def one(window, panels):
        mine = lax.dynamic_slice_in_dim(sources, window * samples, samples, 1)
        mine = lax.all_gather(mine, "win", tiled=True)
        taken = lax.all_gather(mine, "chan")[partner]
        return lax.dynamic_update_slice_in_dim(panels, taken, window * samples, 2)

    empty = jnp.zeros((partner.shape[0], VIRTUAL_SOURCES, sources.shape[1]), sources.dtype)
    return lax.fori_loop(0, windows, one, empty)


def on_device(strain_rate, bandpass_taps, pair_offsets, lag_limit):
    blocks, windows = lax.axis_size("chan"), lax.axis_size("win")
    _, rows, total = strain_rate.shape
    channels = total // (blocks * windows)
    parts = lax.all_to_all(
        strain_rate[0], ("chan", "win"), split_axis=1, concat_axis=0, tiled=True
    ).reshape(blocks, windows, rows, channels)
    receivers, sources = normalize(parts, bandpass_taps)
    offsets = pair_offsets[0]
    used = offsets >= 0
    partner = jnp.where(used, (lax.axis_index("chan") + offsets) % blocks, 0).astype(jnp.int32)
    limit = jnp.where(used, lag_limit[0], -1).astype(jnp.int32)
    if windows > 2:
        lagged = shift(receivers, windows)
        panels = gather_by_window(sources, partner, windows)
        return correlate(lagged, panels, jnp.arange(partner.shape[0], dtype=jnp.int32), limit)
    gathered, lagged = gather_and_shift(sources, receivers, blocks, windows)
    return correlate(lagged, gathered, partner, limit)


def solution(mesh):
    placed = (P("win", "chan", None), P(), P("chan", None), P("chan", None))
    return jax.shard_map(
        on_device,
        mesh=mesh,
        in_specs=placed,
        out_specs=P(None, ("chan", "win"), None),
        check_vma=False,
    )
```

profile of v0, /device:TPU:3, one launch (start us, length us, event | category | flops | bytes accessed | tf_op | source)
XLA Modules:
  0.0 137.2 jit_solution(8416801341518179726)
XLA Ops:
  0.0 1.5 %copy.6 = bf16[8,8,32,256]{3,2,1,0:T(8,128)(2,1)S(1)} copy(bf16[8,8,32,256]{3,1,2,0:T(8,128)(2,1)} %bitcast.22) | data formatting | bytes 2097152
  1.5 1.6 %copy.5 = bf16[64,32,256]{2,0,1:T(8,128)(2,1)} copy(bf16[64,32,256]{2,1,0:T(8,128)(2,1)S(1)} %bitcast.21) | data formatting | bytes 2097152 | tf_op jit(solution)/shard_map/all_to_all | solution.py:385
  3.0 6.4 %all-to-all-start = ((bf16[64,32,256]{2,0,1:T(8,128)(2,1)}), bf16[64,32,256]{2,0,1:T(8,128)(2,1)S(1)}, u32[]{:S(2)}, u32[]{:S(2)}) async-start(bf16[64,32,256]{2,0,1:T(8,128)(2,1)} %copy.5), calls=%async_computation | async-start | bytes 2097152 | tf_op jit(solution)/shard_map/all_to_all | solution.py:385
  9.5 0.7 pad_convert_fusion
  10.2 0.6 reshape.17.taps_ref
  10.8 1.3 bitcast_select_fusion
  12.0 23.6 %all-to-all-done = bf16[64,32,256]{2,0,1:T(8,128)(2,1)S(1)} async-done(((bf16[64,32,256]{2,0,1:T(8,128)(2,1)}), bf16[64,32,256]{2,0,1:T(8,128)(2,1)S(1)}, u32[]{:S(2)}, u32[]{:S(2)}) %all-to-all-start) | async-done | bytes 1048608 | tf_op jit(solution)/shard_map/all_to_all | solution.py:385
  35.7 0.0 copy-start
  35.7 1.0 copy-done
  36.6 5.8 %normalize.1 = (bf16[256,2048]{1,0:T(8,128)(2,1)}, bf16[64,2048]{1,0:T(8,128)(2,1)}) custom-call(f32[1,384]{1,0:T(1,128)} %reshape.17.taps_ref, bf16[16,2,64,256]{3,2,1,0:T(8,128)(2,1)} %bitcast.20), custom_call_target="tpu_custom_call" | custom-call | tf_op jit(solution)/shard_map/normalize/pallas_call | solution.py:72
  42.4 70.2 %gather_and_shift.1 = (bf16[32,64,2048]{2,1,0:T(8,128)(2,1)}, bf16[17,256,2048]{2,1,0:T(8,128)(2,1)}) custom-call(bf16[64,2048]{1,0:T(8,128)(2,1)} %get-tuple-element.9.src_ref, bf16[256,2048]{1,0:T(8,128)(2,1)} %get-tuple-element.10.x_ref), custom_call_target="tpu_custom_call" | custom-call | tf_op jit(solution)/shard_map/gather_and_shift/pallas_call | solution.py:277
  112.6 24.6 %correlate.1 = f32[6,256,2176]{2,1,0:T(8,128)} custom-call(s32[6]{0:T(128)} %get-tuple-element.14.partner, s32[6]{0:T(128)} %get-tuple-element.13.limit, bf16[17,256,2048]{2,1,0:T(8,128)(2,1)} %get-tuple-element.11.lhs_ref, bf16[16,128,2048]{2,1,0:T(8,128)(2,1)} %bitcast.14, bf16[16,128,2048]{2,1,0:T(8,128)(2,1)} %bitcast.15, ...), custom_call_target="tpu_custom_call" | custom-call | tf_op jit(solution)/shard_map/correlate/pallas_call | solution.py:350
Async XLA Ops:
  3.0 32.6 %all-to-all-start = ((bf16[64,32,256]{2,0,1:T(8,128)(2,1)}), bf16[64,32,256]{2,0,1:T(8,128)(2,1)S(1)}, u32[]{:S(2)}, u32[]{:S(2)}) async-start(bf16[64,32,256]{2,0,1:T(8,128)(2,1)} %copy.5), calls=%async_computation | async-start | bytes 2097152 | tf_op jit(solution)/shard_map/all_to_all | solution.py:385
  35.7 1.0 copy-start
where the time goes:
time: 136 us; the launch traced here: 137 us
  Pallas kernels  101 us (74%)
  waiting for transfers between devices  23.6 us (17%)
  starting transfers between devices  6.44 us (5%)
  local copies, waits for them, and re-layouts  4.6 us (3%)
  other arithmetic  1.92 us (1%)
    pallas_call x1, Pallas kernels, gather_and_shift(): pl.pallas_call(functools.partial(gather_kernel, line, windows), out_shape...  70.2 us
    pallas_call x1, Pallas kernels, correlate(): pl.pallas_call(functools.partial(correlate_kernel, 1.0 / math.sqrt(length...  24.6 us
    all_to_all x1, waiting for transfers between devices, on_device(): lax.all_to_all(strain_rate[0], ('chan', 'win'), split_axis=1, concat_axis...  23.6 us
    all_to_all x1, starting transfers between devices, on_device(): lax.all_to_all(strain_rate[0], ('chan', 'win'), split_axis=1, concat_axis...  6.44 us
    pallas_call x1, Pallas kernels, normalize(): pl.pallas_call(functools.partial(normalize_kernel, half), grid=(windows,)...  5.77 us
  transfers between devices with their start and end apart: 1, of which 1 were waited for; matrix products, arithmetic and copies ran while one was open for 2% of the time, Pallas kernels for 0%

commit v1 on v0

--- a/solution.py
+++ b/solution.py
@@ -229,33 +229,45 @@
     for target in (first, second, sibling):
         send(target, own, None, own=True)
     mine.start()
-    levels = [(z, None)]
+    groups = [[(z, None, None, None)]]
     for r in range(1, line):
-        levels += [(z - r, z >= r), (z + r, z + r < line)]
-    done = 0
-    for index, (level, present) in enumerate(levels):
-        if index > 0:
+        groups.append([(z - r, z >= r, up, has_up), (z + r, z + r < line, down, has_down)])
+
+    def from_level(group):
+        for level, present, target, further in group:
             number = block(level, x, core, win)
             when(present, functools.partial(arrived, number))
-            if index % 2 == 1:
-                onward = jnp.logical_and(present, has_up)
-                send(up, number, onward)
-            else:
-                onward = jnp.logical_and(present, has_down)
-                send(down, number, onward)
+            send(target, number, jnp.logical_and(present, further))
             for target in (first, second, sibling):
                 send(target, number, present)
-        for step, (px, pwin) in enumerate(
-            [(first_x, first_win), (second_x, second_win), (1 - x, 1 - win)]
-        ):
-            if done < chunks:
-                lax.fori_loop(done, done + 1, shift_chunk, 0)
-                done += 1
+
+    def from_first(group):
+        for level, present, _, _ in group:
+            number = block(level, first_x, core, first_win)
+            when(present, functools.partial(arrived, number))
+            for target in (second, sibling):
+                send(target, number, present)
+
+    def from_second(group, px, pwin):
+        for level, present, _, _ in group:
             number = block(level, px, core, pwin)
             when(present, functools.partial(arrived, number))
-            if step == 0:
-                send(second, number, present)
             send(sibling, number, present)
+
+    share = chunks // (2 * line)
+    done = 0
+    for k in range(1, line + 2):
+        if k < line:
+            from_level(groups[k])
+        if k <= line:
+            lax.fori_loop(done, done + share, shift_chunk, 0)
+            done += share
+            from_first(groups[k - 1])
+            lax.fori_loop(done, done + share, shift_chunk, 0)
+            done += share
+            from_second(groups[k - 1], second_x, second_win)
+        if k >= 2:
+            from_second(groups[k - 2], 1 - x, 1 - win)
     if done < chunks:
         lax.fori_loop(done, chunks, shift_chunk, 0)
     for level in range(line):

time: 136 us -> 109 us (0.80); the launches traced: 137 us -> 108 us
  Pallas kernels: 101 us -> 71.7 us
    pallas_call x1, Pallas kernels: 70.2 us -> 41.4 us  [gather_and_shift(): pl.pallas_call(functools.partial(gather_kernel, line, windows), out_shape...]
where the time goes in v1:
time: 109 us; the launch traced here: 108 us
  Pallas kernels  71.7 us (66%)
  waiting for transfers between devices  23.6 us (22%)
  starting transfers between devices  6.44 us (6%)
  local copies, waits for them, and re-layouts  4.6 us (4%)
  other arithmetic  1.92 us (2%)
    pallas_call x1, Pallas kernels, gather_and_shift(): pl.pallas_call(functools.partial(gather_kernel, line, windows), out_shape...  41.4 us
    pallas_call x1, Pallas kernels, correlate(): pl.pallas_call(functools.partial(correlate_kernel, 1.0 / math.sqrt(length...  24.6 us
    all_to_all x1, waiting for transfers between devices, on_device(): lax.all_to_all(strain_rate[0], ('chan', 'win'), split_axis=1, concat_axis...  23.6 us
    all_to_all x1, starting transfers between devices, on_device(): lax.all_to_all(strain_rate[0], ('chan', 'win'), split_axis=1, concat_axis...  6.44 us
    pallas_call x1, Pallas kernels, normalize(): pl.pallas_call(functools.partial(normalize_kernel, half), grid=(windows,)...  5.76 us
    unnamed x3, local copies, waits for them, and re-layouts  2.45 us
  transfers between devices with their start and end apart: 1, of which 1 were waited for; matrix products, arithmetic and copies ran while one was open for 2% of the time, Pallas kernels for 0%

profile of v1, /device:TPU:3, one launch (start us, length us, event | category | flops | bytes accessed | tf_op | source)
XLA Modules:
  0.0 108.4 jit_solution(16301491403932107816)
XLA Ops:
  0.0 1.5 %copy.6 = bf16[8,8,32,256]{3,2,1,0:T(8,128)(2,1)S(1)} copy(bf16[8,8,32,256]{3,1,2,0:T(8,128)(2,1)} %bitcast.22) | data formatting | bytes 2097152
  1.5 1.6 %copy.5 = bf16[64,32,256]{2,0,1:T(8,128)(2,1)} copy(bf16[64,32,256]{2,1,0:T(8,128)(2,1)S(1)} %bitcast.21) | data formatting | bytes 2097152 | tf_op jit(solution)/shard_map/all_to_all | solution.py:397
  3.0 6.4 %all-to-all-start = ((bf16[64,32,256]{2,0,1:T(8,128)(2,1)}), bf16[64,32,256]{2,0,1:T(8,128)(2,1)S(1)}, u32[]{:S(2)}, u32[]{:S(2)}) async-start(bf16[64,32,256]{2,0,1:T(8,128)(2,1)} %copy.5), calls=%async_computation | async-start | bytes 2097152 | tf_op jit(solution)/shard_map/all_to_all | solution.py:397
  9.5 0.7 pad_convert_fusion
  10.2 0.6 reshape.17.taps_ref
  10.8 1.3 %bitcast_select_fusion = (s32[6]{0:T(128)}, s32[6]{0:T(128)}) fusion(s32[1,6]{1,0:T(1,128)} %param.6, s32[1,6]{1,0:T(1,128)} %param.7, s32[]{:T(128)S(6)} %axis_index.15), kind=kLoop, calls=%fused_computation.2 | loop fusion | flops 90 | bytes 100 | tf_op jit(solution)/shard_map/jit(_where)/select_n | solution.py:404
  12.0 23.6 %all-to-all-done = bf16[64,32,256]{2,0,1:T(8,128)(2,1)S(1)} async-done(((bf16[64,32,256]{2,0,1:T(8,128)(2,1)}), bf16[64,32,256]{2,0,1:T(8,128)(2,1)S(1)}, u32[]{:S(2)}, u32[]{:S(2)}) %all-to-all-start) | async-done | bytes 1048608 | tf_op jit(solution)/shard_map/all_to_all | solution.py:397
  35.7 0.0 copy-start
  35.7 1.0 copy-done
  36.6 5.8 %normalize.1 = (bf16[256,2048]{1,0:T(8,128)(2,1)}, bf16[64,2048]{1,0:T(8,128)(2,1)}) custom-call(f32[1,384]{1,0:T(1,128)} %reshape.17.taps_ref, bf16[16,2,64,256]{3,2,1,0:T(8,128)(2,1)} %bitcast.20), custom_call_target="tpu_custom_call" | custom-call | tf_op jit(solution)/shard_map/normalize/pallas_call | solution.py:72
  42.4 41.4 %gather_and_shift.1 = (bf16[32,64,2048]{2,1,0:T(8,128)(2,1)}, bf16[17,256,2048]{2,1,0:T(8,128)(2,1)}) custom-call(bf16[64,2048]{1,0:T(8,128)(2,1)} %get-tuple-element.9.src_ref, bf16[256,2048]{1,0:T(8,128)(2,1)} %get-tuple-element.10.x_ref), custom_call_target="tpu_custom_call" | custom-call | tf_op jit(solution)/shard_map/gather_and_shift/pallas_call | solution.py:289
  83.8 24.6 %correlate.1 = f32[6,256,2176]{2,1,0:T(8,128)} custom-call(s32[6]{0:T(128)} %get-tuple-element.14.partner, s32[6]{0:T(128)} %get-tuple-element.13.limit, bf16[17,256,2048]{2,1,0:T(8,128)(2,1)} %get-tuple-element.11.lhs_ref, bf16[16,128,2048]{2,1,0:T(8,128)(2,1)} %bitcast.14, bf16[16,128,2048]{2,1,0:T(8,128)(2,1)} %bitcast.15, ...), custom_call_target="tpu_custom_call" | custom-call | tf_op jit(solution)/shard_map/correlate/pallas_call | solution.py:362
Async XLA Ops:
  3.0 32.6 %all-to-all-start = ((bf16[64,32,256]{2,0,1:T(8,128)(2,1)}), bf16[64,32,256]{2,0,1:T(8,128)(2,1)S(1)}, u32[]{:S(2)}, u32[]{:S(2)}) async-start(bf16[64,32,256]{2,0,1:T(8,128)(2,1)} %copy.5), calls=%async_computation | async-start | bytes 2097152 | tf_op jit(solution)/shard_map/all_to_all | solution.py:397
  35.7 1.0 copy-start

commit v2 on v1

--- a/solution.py
+++ b/solution.py
@@ -23,22 +23,17 @@
     return pltpu.roll(wide, 0, 1, stride=1, stride_axis=0).astype(jnp.bfloat16)
 
 
-def normalize_kernel(half, taps_ref, x_ref, out_ref, src_ref, padded, level, filtered):
-    parts, _, rows, channels = x_ref.shape
-    samples = parts * rows
+def clean(half, taps, box, parts, out_ref, src_ref, padded, level, filtered):
+    rows, channels = parts[0].shape
+    samples = len(parts) * rows
     tap_count = 2 * half + 1
     tail = padded.shape[0] - samples - half
     padded[:half] = jnp.zeros((half, channels), jnp.bfloat16)
     padded[half + samples :] = jnp.zeros((tail, channels), jnp.bfloat16)
     level[:half] = jnp.zeros((half, channels), jnp.bfloat16)
     level[half + samples :] = jnp.zeros((tail, channels), jnp.bfloat16)
-    for i in range(parts):
-        padded[half + i * rows : half + (i + 1) * rows] = x_ref[i, 0]
-    taps = band(taps_ref[...], half)
-    ones = jnp.where(
-        lax.broadcasted_iota(jnp.int32, (1, REACH), 1) < tap_count, 1.0, 0.0
-    ).astype(jnp.float32)
-    box = band(ones, half)
+    for i, part in enumerate(parts):
+        padded[half + i * rows : half + (i + 1) * rows] = part[...]
     for p in range(samples // PIECE):
         low = p * PIECE
         value = jnp.dot(taps, padded[low : low + REACH], preferred_element_type=jnp.float32)
@@ -63,6 +58,19 @@
         ).astype(jnp.bfloat16)
 
 
+def bands(half, taps_ref):
+    ones = jnp.where(
+        lax.broadcasted_iota(jnp.int32, (1, REACH), 1) < 2 * half + 1, 1.0, 0.0
+    ).astype(jnp.float32)
+    return band(taps_ref[...], half), band(ones, half)
+
+
+def normalize_kernel(half, taps_ref, x_ref, out_ref, src_ref, padded, level, filtered):
+    taps, box = bands(half, taps_ref)
+    parts = [x_ref.at[i, 0] for i in range(x_ref.shape[0])]
+    clean(half, taps, box, parts, out_ref, src_ref, padded, level, filtered)
+
+
 def normalize(parts, taps):
     blocks, windows, rows, channels = parts.shape
     samples = blocks * rows
@@ -92,6 +100,120 @@
         compiler_params=pltpu.CompilerParams(vmem_limit_bytes=VMEM_LIMIT),
         name="normalize",
     )(row, parts)
+
+
+def exchange_kernel(
+    half, windows, taps_ref, x_ref, out_ref, src_ref, parts, padded, level, filtered, own_sem,
+    send_sem, recv_sem
+):
+    chan, win = lax.axis_index("chan"), lax.axis_index("win")
+    devices, rows, channels = parts.shape
+    me = chan * windows + win
+
+    def place(number):
+        return (number // windows, number % windows)
+
+    def copy(step):
+        target = (me + step) % devices
+        low = pl.multiple_of(target * channels, channels)
+        return pltpu.make_async_remote_copy(
+            src_ref=x_ref.at[:, pl.ds(low, channels)],
+            dst_ref=parts.at[me],
+            send_sem=send_sem.at[step],
+            recv_sem=recv_sem.at[me],
+            device_id=place(target),
+            device_id_type=pl.DeviceIdType.MESH,
+        )
+
+    def greet(step, carry):
+        pl.semaphore_signal(
+            barrier,
+            inc=1,
+            device_id=place((me + step) % devices),
+            device_id_type=pl.DeviceIdType.MESH,
+        )
+        return carry
+
+    def start(step, carry):
+        copy(step).start()
+        return carry
+
+    def arrive(step, carry):
+        number = (me + step) % devices
+        pltpu.make_async_remote_copy(
+            src_ref=parts.at[number],
+            dst_ref=parts.at[number],
+            send_sem=send_sem.at[0],
+            recv_sem=recv_sem.at[number],
+            device_id=place(number),
+            device_id_type=pl.DeviceIdType.MESH,
+        ).wait_recv()
+        return carry
+
+    def leave(step, carry):
+        copy(step).wait_send()
+        return carry
+
+    barrier = pltpu.get_barrier_semaphore()
+    lax.fori_loop(1, devices, greet, 0)
+    pl.semaphore_wait(barrier, devices - 1)
+    lax.fori_loop(1, devices, start, 0)
+    mine = pltpu.make_async_copy(
+        x_ref.at[:, pl.ds(pl.multiple_of(me * channels, channels), channels)],
+        parts.at[me],
+        own_sem,
+    )
+    mine.start()
+    taps, box = bands(half, taps_ref)
+    mine.wait()
+    lax.fori_loop(1, devices, arrive, 0)
+    for w in range(windows):
+        samples = devices // windows * rows
+        along = pl.ds(w * samples, samples)
+        clean(
+            half,
+            taps,
+            box,
+            [parts.at[i * windows + w] for i in range(devices // windows)],
+            out_ref.at[:, along],
+            src_ref.at[:, along],
+            padded,
+            level,
+            filtered,
+        )
+    lax.fori_loop(1, devices, leave, 0)
+
+
+def exchange_and_normalize(strain, taps, blocks, windows):
+    devices = blocks * windows
+    rows, total = strain.shape
+    channels, samples = total // devices, blocks * rows
+    half = (taps.shape[0] - 1) // 2
+    sources = VIRTUAL_SOURCES // windows
+    row = jnp.pad(taps.astype(jnp.float32), (0, REACH - taps.shape[0]))[None]
+    vmem = pl.BlockSpec(memory_space=pltpu.VMEM)
+    return pl.pallas_call(
+        functools.partial(exchange_kernel, half, windows),
+        out_shape=(
+            jax.ShapeDtypeStruct((channels, windows * samples), jnp.bfloat16),
+            jax.ShapeDtypeStruct((sources, windows * samples), jnp.bfloat16),
+        ),
+        in_specs=[vmem, pl.BlockSpec(memory_space=pl.ANY)],
+        out_specs=(vmem, vmem),
+        scratch_shapes=[
+            pltpu.VMEM((devices, rows, channels), jnp.bfloat16),
+            pltpu.VMEM((samples + REACH - PIECE, channels), jnp.bfloat16),
+            pltpu.VMEM((samples + REACH - PIECE, channels), jnp.bfloat16),
+            pltpu.VMEM((samples, channels), jnp.float32),
+            pltpu.SemaphoreType.DMA,
+            pltpu.SemaphoreType.DMA((devices,)),
+            pltpu.SemaphoreType.DMA((devices,)),
+        ],
+        compiler_params=pltpu.CompilerParams(
+            collective_id=1, has_side_effects=True, vmem_limit_bytes=VMEM_LIMIT
+        ),
+        name="exchange_and_normalize",
+    )(row, strain)
 
 
 def moved_rows(value, spot, lag):
@@ -394,10 +516,15 @@
     blocks, windows = lax.axis_size("chan"), lax.axis_size("win")
     _, rows, total = strain_rate.shape
     channels = total // (blocks * windows)
-    parts = lax.all_to_all(
-        strain_rate[0], ("chan", "win"), split_axis=1, concat_axis=0, tiled=True
-    ).reshape(blocks, windows, rows, channels)
-    receivers, sources = normalize(parts, bandpass_taps)
+    if windows > 2:
+        parts = lax.all_to_all(
+            strain_rate[0], ("chan", "win"), split_axis=1, concat_axis=0, tiled=True
+        ).reshape(blocks, windows, rows, channels)
+        receivers, sources = normalize(parts, bandpass_taps)
+    else:
+        receivers, sources = exchange_and_normalize(
+            strain_rate[0], bandpass_taps, blocks, windows
+        )
     offsets = pair_offsets[0]
     used = offsets >= 0
     partner = jnp.where(used, (lax.axis_index("chan") + offsets) % blocks, 0).astype(jnp.int32)

time: 109 us -> 107 us (0.982)
  the two profiles are of different devices: /device:TPU:3 before, /device:TPU:1 now
where the time goes in v2:
time: 107 us
  Pallas kernels  105 us (98%)
  other arithmetic  1.87 us (2%)
    pallas_call x1, Pallas kernels, gather_and_shift(): pl.pallas_call(functools.partial(gather_kernel, line, windows), out_shape...  52 us
    pallas_call x1, Pallas kernels, exchange_and_normalize(): pl.pallas_call(functools.partial(exchange_kernel, half, windows), out_sha...  28.4 us
    pallas_call x1, Pallas kernels, correlate(): pl.pallas_call(functools.partial(correlate_kernel, 1.0 / math.sqrt(length...  24.6 us

profile of v2, /device:TPU:1, one launch (start us, length us, event | category | flops | bytes accessed | tf_op | source)
XLA Modules:
  0.0 107.4 jit_solution(13114253296010606517)
XLA Ops:
  0.0 1.2 %bitcast_select_fusion = (s32[6]{0:T(128)}, s32[6]{0:T(128)}) fusion(s32[1,6]{1,0:T(1,128)} %param.6, s32[1,6]{1,0:T(1,128)} %param.7, s32[]{:T(128)S(6)} %axis_index.15), kind=kLoop, calls=%fused_computation.2 | loop fusion | flops 90 | bytes 100 | tf_op jit(solution)/shard_map/jit(_where)/select_n | solution.py:531
  1.2 0.7 pad_convert_fusion
  1.9 0.6 reshape.8.taps_ref
  2.4 28.4 %exchange_and_normalize.1 = (bf16[256,2048]{1,0:T(8,128)(2,1)}, bf16[64,2048]{1,0:T(8,128)(2,1)}) custom-call(f32[1,384]{1,0:T(1,128)} %reshape.8.taps_ref, bf16[64,8192]{1,0:T(8,128)(2,1)} %bitcast.15), custom_call_target="tpu_custom_call" | custom-call | tf_op jit(solution)/shard_map/exchange_and_normalize/pallas_call | solution.py:195
  30.9 52.0 %gather_and_shift.1 = (bf16[32,64,2048]{2,1,0:T(8,128)(2,1)}, bf16[17,256,2048]{2,1,0:T(8,128)(2,1)}) custom-call(bf16[64,2048]{1,0:T(8,128)(2,1)} %get-tuple-element.9.src_ref, bf16[256,2048]{1,0:T(8,128)(2,1)} %get-tuple-element.10.x_ref), custom_call_target="tpu_custom_call" | custom-call | tf_op jit(solution)/shard_map/gather_and_shift/pallas_call | solution.py:411
  82.8 24.6 %correlate.1 = f32[6,256,2176]{2,1,0:T(8,128)} custom-call(s32[6]{0:T(128)} %get-tuple-element.14.partner, s32[6]{0:T(128)} %get-tuple-element.13.limit, bf16[17,256,2048]{2,1,0:T(8,128)(2,1)} %get-tuple-element.11.lhs_ref, bf16[16,128,2048]{2,1,0:T(8,128)(2,1)} %bitcast.9, bf16[16,128,2048]{2,1,0:T(8,128)(2,1)} %bitcast.10, ...), custom_call_target="tpu_custom_call" | custom-call | tf_op jit(solution)/shard_map/correlate/pallas_call | solution.py:484
